TPU v7x, 256 devices: a whole 4x4x8 slice. The times are simulated.
256 devices in a mesh: gx: 16 (over y, x_lo, core), gy: 16 (over z, x_hi).
Axes of the slice: x: 4 (x_hi: 2, x_lo: 2; x = x_hi * 2 + x_lo), y: 4, z: 8, core: 2. Of those that a mesh axis runs over, the one named last changes fastest.
Arguments:
- features: bfloat16 [65536, 128], P(('gx', 'gy')), may hold values from -6 to 6
- w_sub: bfloat16 [27, 128, 128], replicated, may hold values from -0.1875 to 0.1875
- w_down: bfloat16 [1024, 256], replicated, may hold values from -0.25 to 0.25
- cell_ids: int32 [65536], P(('gx', 'gy')), may hold values from -1 to 511, as said below
- send_rows: int32 [73728], P(('gx', 'gy')), may hold values from 0 to 256, as said below
- map_in: int32 [27, 65536], P(None, ('gx', 'gy')), may hold values from 0 to 608, as said below
- map_out: int32 [27, 65536], P(None, ('gx', 'gy')), may hold values from 0 to 256, as said below
- cotangent: bfloat16 [16384, 256], P(('gx', 'gy')), may hold values from -6 to 6
Outputs:
- coarse: bfloat16 [16384, 256], P(('gx', 'gy'))
- feature_grad: bfloat16 [65536, 128], P(('gx', 'gy'))
- sub_grad: float32 [27, 128, 128], replicated
- down_grad: float32 [1024, 256], replicated
Inputs may be any that keep to these rules, and one draw needn't show every extreme that they name: `cell_ids`: in every region the used rows are 0 to count - 1, in increasing cell number; -1 marks unused rows; a region uses at most 256 rows and some region uses exactly 256. `send_rows`: the row of the voxel at each rim cell, 256 where the cell is empty; rim cells listed in increasing cell number. `map_in`: indices into lookup_table: below 256 own rows, 257 + g ghost row g; within each offset the pairs come in increasing output row, and unused entries stand at the end with the value 256. A pair exists exactly where the output voxel and the voxel at its offset both exist. `map_out`: the output row of each pair; 256 on unused entries at the end of each offset's list; each row appears at most once per offset.
All inputs are finite; a program needn't handle non-finite values.
Results may differ from a plain program's by a relative error of at most 0.015.
Values may be sent and summed in bfloat16 or wider, within the bound.
No kernel may reach another device: no remote copies, remote signals or barrier semaphores. Data moves between devices by JAX's collectives and lax.ppermute only.
A program may use at most 64 MiB of HBM per device.

v0:
```python
import jax
import jax.numpy as jnp
import numpy as np
from jax import lax
from jax.sharding import PartitionSpec as P

LX = 4
LY = 16
LZ = 8
U_DEV = 64


def shifted(value, axis, by):
    peers = lax.axis_size(axis)
    pairs = [(i, i + by) for i in range(peers) if 0 <= i + by < peers]
    return lax.ppermute(value, axis, pairs)


def with_halo(block, sides, width):
    for axis, dim in sides:
        count = lax.axis_size(axis)
        forward = [(i, i + 1) for i in range(count - 1)]
        backward = [(target, source) for source, target in forward]
        low = lax.ppermute(
            lax.slice_in_dim(block, block.shape[dim] - width, None, axis=dim), axis, forward
        )
        high = lax.ppermute(lax.slice_in_dim(block, 0, width, axis=dim), axis, backward)
        block = jnp.concatenate([low, block, high], axis=dim)
    return block


def frame_tables():
    cell_count = LX * LY * LZ
    cell_index = np.arange(cell_count)
    coord_x = cell_index // (LY * LZ)
    coord_y = cell_index // LZ % LY
    on_rim = (coord_x == 0) | (coord_x == LX - 1) | (coord_y == 0) | (coord_y == LY - 1)
    rim_place = np.full(cell_count, -1, np.int64)
    rim_place[on_rim] = np.arange(int(on_rim.sum()))
    depth_range = np.arange(LZ)
    neighbour_list, face_list, side_list = ([], [], [])
    for frame_x in range(-1, LX + 1):
        for frame_y in range(-1, LY + 1):
            if 0 <= frame_x < LX and 0 <= frame_y < LY:
                continue
            step_x = -1 if frame_x < 0 else 1 if frame_x >= LX else 0
            step_y = -1 if frame_y < 0 else 1 if frame_y >= LY else 0
            local_cell = ((frame_x - step_x * LX) * LY + (frame_y - step_y * LY)) * LZ + depth_range
            neighbour_list.append(np.full(LZ, (step_x + 1) * 3 + step_y + 1))
            face_list.append(rim_place[local_cell])
            if 0 <= frame_y < LY:
                first_place = (0 if frame_x < 0 else LY * LZ) + frame_y * LZ
            else:
                column = frame_x if 0 <= frame_x < LX else LX if frame_x < 0 else LX + 1
                first_place = 2 * LY * LZ + (0 if frame_y < 0 else (LX + 2) * LZ) + column * LZ
            side_list.append(first_place + depth_range)
    side_place = np.concatenate(side_list)

    def face_rows(spots):
        return np.concatenate(
            [rim_place[(spot_x * LY + spot_y) * LZ + depth_range] for spot_x, spot_y in spots]
        )

    return {
        "neighbour": np.concatenate(neighbour_list),
        "face": np.concatenate(face_list),
        "side_place": side_place,
        "side_order": np.argsort(side_place),
        "x_high": face_rows([(LX - 1, column_y) for column_y in range(LY)]),
        "x_low": face_rows([(0, column_y) for column_y in range(LY)]),
        "y_high": face_rows([(column_x, LY - 1) for column_x in range(LX)]),
        "y_low": face_rows([(column_x, 0) for column_x in range(LX)]),
    }


def assemble_grid(interior, ghost_rows):
    channels = interior.shape[-1]
    top_len = (LY + 2) * LZ
    top_plane = ghost_rows[:top_len].reshape(1, LY + 2, LZ, channels)
    side_cols = ghost_rows[top_len : top_len + 2 * LX * LZ].reshape(LX, 2, LZ, channels)
    bottom_plane = ghost_rows[top_len + 2 * LX * LZ :].reshape(1, LY + 2, LZ, channels)
    middle = jnp.concatenate([side_cols[:, :1], interior, side_cols[:, 1:]], 1)
    return jnp.concatenate([top_plane, middle, bottom_plane], 0)


def frame_of(grid):
    channels = grid.shape[-1]
    side_cols = jnp.stack([grid[1:-1, 0], grid[1:-1, -1]], 1)
    return jnp.concatenate(
        [
            grid[0].reshape(-1, channels),
            side_cols.reshape(-1, channels),
            grid[-1].reshape(-1, channels),
        ],
        0,
    )


def shifted_columns(padded, start_x, start_y, span_x, span_y, starts_z):
    channels = padded.shape[-1]
    slab = padded[start_x : start_x + span_x, start_y : start_y + span_y]
    columns = jnp.concatenate([slab[:, :, start_z : start_z + LZ] for start_z in starts_z], -1)
    return columns.reshape(span_x * span_y * LZ, 3 * channels)


def return_along_y(piece, step):
    return shifted(piece, "gy", step)


def return_along_x(piece, step):
    return shifted(piece, "gx", step)


def local(features, w_sub, w_down, cell_ids, send_rows, map_in, map_out, cotangent):
    frames = frame_tables()
    row_count, channels = features.shape
    cell_count = LX * LY * LZ
    zero_row = jnp.zeros((1, channels), jnp.bfloat16)
    padded = jnp.concatenate([features, zero_row], 0)
    rim_rows = padded[send_rows]
    face_count = rim_rows.shape[0]
    plane_x = LY * LZ
    plane_y = (LX + 2) * LZ
    inner_y = LX * LZ
    beside_all = with_halo(rim_rows[None, None], (("gx", 0), ("gy", 1)), 1)
    flat_rows = beside_all.reshape(9 * face_count, channels)
    ghost_rows = flat_rows[
        jnp.asarray(frames["neighbour"] * face_count + frames["face"], jnp.int32)
    ]
    cell_slot = jnp.where(cell_ids >= 0, cell_ids, cell_count)
    dense_flat = (
        jnp.zeros((cell_count + 1, channels), jnp.bfloat16).at[cell_slot].set(features)[:cell_count]
    )
    active = jnp.zeros((cell_count + 1, 1), jnp.float32).at[cell_slot].set(1.0)[:cell_count]
    active = active.reshape(LX, LY, LZ, 1)
    grid = assemble_grid(dense_flat.reshape(LX, LY, LZ, channels), ghost_rows)
    grid = jnp.pad(grid, ((0, 0), (0, 0), (1, 1), (0, 0)))
    pre_act = jnp.zeros((cell_count, channels), jnp.float32)
    for step_x in range(3):
        for step_y in range(3):
            first = step_x * 9 + step_y * 3
            columns = shifted_columns(grid, step_x, step_y, LX, LY, (0, 1, 2))
            kernel = w_sub[first : first + 3].reshape(3 * channels, channels)
            pre_act = pre_act + jnp.dot(columns, kernel, preferred_element_type=jnp.float32)
    pre_act = pre_act.reshape(LX, LY, LZ, channels)
    hidden = (jax.nn.silu(pre_act) * active).astype(jnp.bfloat16)
    coarse_input = hidden.reshape(LX // 2, 2, LY // 2, 2, LZ // 2, 2, channels).transpose(
        0, 2, 4, 1, 3, 5, 6
    )
    coarse_input = coarse_input.reshape(U_DEV, 8 * channels)
    coarse = jnp.dot(coarse_input, w_down, preferred_element_type=jnp.float32).astype(jnp.bfloat16)
    back_rows = lax.dot_general(
        cotangent, w_down, (((1,), (1,)), ((), ())), preferred_element_type=jnp.float32
    ).astype(jnp.bfloat16)
    hidden_grad = back_rows.reshape(LX // 2, LY // 2, LZ // 2, 2, 2, 2, channels).transpose(
        0, 3, 1, 4, 2, 5, 6
    )
    hidden_grad = hidden_grad.reshape(LX, LY, LZ, channels)
    sigmoid_value = jax.nn.sigmoid(pre_act)
    pre_grad = (
        hidden_grad.astype(jnp.float32)
        * sigmoid_value
        * (1.0 + pre_act * (1.0 - sigmoid_value))
        * active
    ).astype(jnp.bfloat16)
    down_local = lax.dot_general(
        coarse_input, cotangent, (((0,), (0,)), ((), ())), preferred_element_type=jnp.float32
    )
    grad_flat = pre_grad.reshape(cell_count, channels)
    grad_padded = jnp.pad(pre_grad, ((2, 2), (2, 2), (1, 1), (0, 0)))
    weight_parts = []
    table_dense = jnp.zeros(((LX + 2) * (LY + 2) * LZ, channels), jnp.float32)
    for step_x in range(3):
        for step_y in range(3):
            first = step_x * 9 + step_y * 3
            columns = shifted_columns(grid, step_x, step_y, LX, LY, (0, 1, 2))
            part_grad = lax.dot_general(
                columns, grad_flat, (((0,), (0,)), ((), ())), preferred_element_type=jnp.float32
            )
            weight_parts.append(part_grad.reshape(3, channels, channels))
            back_columns = shifted_columns(
                grad_padded, 2 - step_x, 2 - step_y, LX + 2, LY + 2, (2, 1, 0)
            )
            flipped = jnp.swapaxes(w_sub[first : first + 3], 1, 2).reshape(3 * channels, channels)
            table_dense = table_dense + jnp.dot(
                back_columns, flipped, preferred_element_type=jnp.float32
            )
    sub_local = jnp.concatenate(weight_parts, 0)
    table_dense = table_dense.reshape(LX + 2, LY + 2, LZ, channels)
    sub_grad, down_grad = lax.psum((sub_local, down_local), ("gx", "gy"))
    ghost_grad = frame_of(table_dense)
    side_grad = ghost_grad[jnp.asarray(frames["side_order"], jnp.int32)]
    grad_west = side_grad[:plane_x]
    grad_east = side_grad[plane_x : 2 * plane_x]
    grad_south = side_grad[2 * plane_x : 2 * plane_x + plane_y]
    grad_north = side_grad[2 * plane_x + plane_y :]
    return_high = return_along_y(grad_south, -1)
    return_low = return_along_y(grad_north, 1)
    grad_west = (
        grad_west.at[(LY - 1) * LZ :]
        .add(return_high[inner_y : inner_y + LZ])
        .at[:LZ]
        .add(return_low[inner_y : inner_y + LZ])
    )
    grad_east = (
        grad_east.at[(LY - 1) * LZ :]
        .add(return_high[inner_y + LZ :])
        .at[:LZ]
        .add(return_low[inner_y + LZ :])
    )
    return_east = return_along_x(grad_west, -1)
    return_west = return_along_x(grad_east, 1)
    rim_grad = jnp.zeros((face_count, channels), jnp.float32)
    rim_grad = rim_grad.at[frames["x_high"]].add(return_east).at[frames["x_low"]].add(return_west)
    rim_grad = (
        rim_grad.at[frames["y_high"]]
        .add(return_high[:inner_y])
        .at[frames["y_low"]]
        .add(return_low[:inner_y])
    )
    interior_grad = table_dense[1:-1, 1:-1].reshape(cell_count, channels)
    interior_grad = jnp.concatenate([interior_grad, jnp.zeros((1, channels), jnp.float32)], 0)
    own_grad = interior_grad[cell_slot]
    own_grad = (
        jnp.concatenate([own_grad, jnp.zeros((1, channels), jnp.float32)], 0)
        .at[send_rows]
        .add(rim_grad)[:row_count]
    )
    feature_grad = own_grad.astype(jnp.bfloat16)
    return (coarse, feature_grad, sub_grad, down_grad)


def solution(mesh):
    placed = (
        P(("gx", "gy"), None),
        P(),
        P(),
        P(("gx", "gy")),
        P(("gx", "gy")),
        P(None, ("gx", "gy")),
        P(None, ("gx", "gy")),
        P(("gx", "gy"), None),
    )
    return jax.shard_map(
        local,
        mesh=mesh,
        in_specs=placed,
        out_specs=(P(("gx", "gy"), None), P(("gx", "gy"), None), P(), P()),
        check_vma=False,
    )
```

profile of v0, /device:TPU:2, one launch (start us, length us, event | category | flops | bytes accessed | tf_op | source)
XLA Modules:
  0.0 361.6 jit_solution(8910161390339559812)
XLA Ops:
  9.3 1.4 gather_fusion
  10.7 1.9 collective-permute-start.1
  12.6 2.4 collective-permute-start
  15.1 2.4 slice_bitcast_fusion.2
  17.7 1.4 scatter_custom_fusion.1
  20.1 1.5 scatter_custom_fusion
  29.7 1.3 collective-permute-start.3
  31.0 6.2 %collective-permute-start.2 = (bf16[3,1,288,128]{3,2,1,0:T(8,128)(2,1)S(1)}, bf16[3,1,288,128]{3,2,1,0:T(8,128)(2,1)S(1)}, u32[]{:S(2)}, u32[]{:S(2)}) collective-permute-start(bf16[3,1,288,128]{3,2,1,0:T(8,128)(2,1)S(1)} %pad_maximum_fusion.19), channel_id=1, source_target_pairs={{0,1},{1,2},{2,3},{3,4},{4,5},{5,6},{6,7},{7,8},{8,9},{9,10},{10,1... | collective-permute-start | bytes 663560 | tf_op jit(solution)/shard_map/ppermute | solution.py:24
  37.9 2.5 collective-permute-done.3
  40.4 4.7 %collective-permute-done.2 = bf16[3,1,288,128]{3,2,1,0:T(8,128)(2,1)S(1)} collective-permute-done((bf16[3,1,288,128]{3,2,1,0:T(8,128)(2,1)S(1)}, bf16[3,1,288,128]{3,2,1,0:T(8,128)(2,1)S(1)}, u32[]{:S(2)}, u32[]{:S(2)}) %collective-permute-start.2) | collective-permute-done | bytes 221216 | tf_op jit(solution)/shard_map/ppermute | solution.py:24
  45.2 1.4 gather_fusion.1
  52.8 1.3 pad_slice_fusion.1
  54.1 2.3 pad_slice_fusion.2
  56.4 1.9 copy.116
  58.3 2.0 copy.112
  61.4 0.9 copy.110
  62.3 0.9 copy.109
  66.2 1.0 copy.113
  67.2 1.3 fusion.47
  80.8 1.2 copy-done.1
  82.1 1.1 gather_fusion.3
  83.2 1.3 collective-permute-start.4
  84.5 6.5 %collective-permute-start.5 = (f32[48,128]{1,0:T(8,128)S(1)}, f32[48,128]{1,0:T(8,128)S(1)}, u32[]{:S(2)}, u32[]{:S(2)}) collective-permute-start(f32[48,128]{1,0:T(8,128)S(1)} %get-tuple-element.104), channel_id=1, source_target_pairs={{0,1},{1,2},{2,3},{3,4},{4,5},{5,6},{6,7},{7,8},{8,9},{9,10},{10,1... | collective-permute-start | bytes 73736 | tf_op jit(solution)/shard_map/ppermute | solution.py:16
  91.1 1.5 collective-permute-done.5
  92.5 1.9 collective-permute-start.7
  94.5 3.6 %collective-permute-start.6 = (f32[128,128]{1,0:T(8,128)S(1)}, f32[128,128]{1,0:T(8,128)S(1)}, u32[]{:S(2)}, u32[]{:S(2)}) collective-permute-start(f32[128,128]{1,0:T(8,128)S(1)} %get-tuple-element.140), channel_id=1, source_target_pairs={{16,0},{32,16},{48,32},{64,48},{80,64},{96,80},{112,96},{128,112},... | collective-permute-start | bytes 196616 | tf_op jit(solution)/shard_map/ppermute | solution.py:16
  100.0 1.1 scatter_custom_fusion.2
  101.2 1.3 scatter_fusion
  104.3 2.1 scatter_fusion.1
  107.1 243.8 %all-reduce.8.cloned.1.call-done = (f32[27,128,128]{2,1,0:T(8,128)}, f32[1024,256]{1,0:T(8,128)}) async-done(((f32[27,128,128]{2,1,0:T(8,128)}, f32[1024,256]{1,0:T(8,128)}), (f32[27,128,128]{2,1,0:T(8,128)}, f32[1024,256]{1,0:T(8,128)})) %all-reduce.8.cloned.1.call-update) | async-done | bytes 2818064 | tf_op jit(solution)/shard_map/psum | solution.py:190
  350.8 3.0 copy.138
  353.8 1.0 copy.139
  (228 shorter events, 38.3 us)
Async XLA Ops:
  7.2 10.3 %copy-start = (bf16[1024,256]{1,0:T(8,128)(2,1)S(1)}, bf16[1024,256]{1,0:T(8,128)(2,1)}, u32[]{:S(2)}) copy-start(bf16[1024,256]{1,0:T(8,128)(2,1)} %param.28) | copy-start | bytes 1572868
  7.2 343.7 %all-reduce.8.cloned.1.call-start = ((), (), s32[]{:S(2)}) async-start(), calls=%async_computation | async-start | bytes 5636096 | tf_op jit(solution)/shard_map/psum | solution.py:190
  10.7 6.7 %copy-start.52 = (bf16[64,256]{1,0:T(8,128)(2,1)S(1)}, bf16[64,256]{1,0:T(8,128)(2,1)}, u32[]{:S(2)}) copy-start(bf16[64,256]{1,0:T(8,128)(2,1)} %param.31) | copy-start | bytes 98308
  10.7 7.0 %copy-start.60 = (s32[256]{0:T(256)S(1)}, s32[256]{0:T(256)}, u32[]{:S(2)}) copy-start(s32[256]{0:T(256)} %param.29) | copy-start | bytes 3076
  10.7 19.0 %collective-permute-start.1 = (bf16[1,1,288,128]{3,2,1,0:T(8,128)(2,1)S(1)}, bf16[1,1,288,128]{3,2,1,0:T(8,128)(2,1)S(1)}, u32[]{:S(2)}, u32[]{:S(2)}) collective-permute-start(bf16[1,1,288,128]{3,2,1,0:T(8,128)(2,1)S(1)} %bitcast.218), channel_id=1, source_target_pairs={{16,0},{32,16},{48,32},{64,48},{80,64},{96,80},{112,96},{128,112},... | collective-permute-start | bytes 221192 | tf_op jit(solution)/shard_map/ppermute | solution.py:27
  12.6 17.0 %collective-permute-start = (bf16[1,1,288,128]{3,2,1,0:T(8,128)(2,1)S(1)}, bf16[1,1,288,128]{3,2,1,0:T(8,128)(2,1)S(1)}, u32[]{:S(2)}, u32[]{:S(2)}) collective-permute-start(bf16[1,1,288,128]{3,2,1,0:T(8,128)(2,1)S(1)} %bitcast.219), channel_id=1, source_target_pairs={{0,16},{16,32},{32,48},{48,64},{64,80},{80,96},{96,112},{112,128},... | collective-permute-start | bytes 221192 | tf_op jit(solution)/shard_map/ppermute | solution.py:24
  22.7 14.6 %copy-start.58 = (s32[352]{0:T(512)S(1)}, s32[352]{0:T(512)}, u32[]{:S(2)}) copy-start(s32[352]{0:T(512)} %constant.171) | copy-start | bytes 4228
  22.7 14.6 %copy-start.59 = (s32[352]{0:T(512)S(1)}, s32[352]{0:T(512)}, u32[]{:S(2)}) copy-start(s32[352]{0:T(512)} %constant.173) | copy-start | bytes 4228
  29.7 10.7 %collective-permute-start.3 = (bf16[3,1,288,128]{3,2,1,0:T(8,128)(2,1)S(1)}, bf16[3,1,288,128]{3,2,1,0:T(8,128)(2,1)S(1)}, u32[]{:S(2)}, u32[]{:S(2)}) collective-permute-start(bf16[3,1,288,128]{3,2,1,0:T(8,128)(2,1)S(1)} %pad_maximum_fusion.19), channel_id=1, source_target_pairs={{1,0},{2,1},{3,2},{4,3},{5,4},{6,5},{7,6},{8,7},{9,8},{10,9},{11,1... | collective-permute-start | bytes 663560 | tf_op jit(solution)/shard_map/ppermute | solution.py:27
  31.0 14.1 %collective-permute-start.2 = (bf16[3,1,288,128]{3,2,1,0:T(8,128)(2,1)S(1)}, bf16[3,1,288,128]{3,2,1,0:T(8,128)(2,1)S(1)}, u32[]{:S(2)}, u32[]{:S(2)}) collective-permute-start(bf16[3,1,288,128]{3,2,1,0:T(8,128)(2,1)S(1)} %pad_maximum_fusion.19), channel_id=1, source_target_pairs={{0,1},{1,2},{2,3},{3,4},{4,5},{5,6},{6,7},{7,8},{8,9},{9,10},{10,1... | collective-permute-start | bytes 663560 | tf_op jit(solution)/shard_map/ppermute | solution.py:24
  50.0 1.6 copy-start.2
  51.3 1.4 copy-start.53
  61.4 1.9 copy-start.14
  65.3 3.2 copy-start.32
  65.3 3.2 copy-start.33
  65.3 3.2 copy-start.41
  67.2 1.5 copy-start.49
  68.6 1.2 copy-start.31
  68.6 1.2 copy-start.36
  68.6 1.3 copy-start.37
  71.1 1.2 copy-start.26
  77.3 1.3 copy-start.7
  77.3 1.5 copy-start.6
  77.7 1.5 copy-start.9
  80.8 1.2 copy-start.1
  80.8 1.3 copy-start.57
  83.2 7.8 %collective-permute-start.4 = (f32[48,128]{1,0:T(8,128)S(1)}, f32[48,128]{1,0:T(8,128)S(1)}, u32[]{:S(2)}, u32[]{:S(2)}) collective-permute-start(f32[48,128]{1,0:T(8,128)S(1)} %get-tuple-element.105), channel_id=1, source_target_pairs={{1,0},{2,1},{3,2},{4,3},{5,4},{6,5},{7,6},{8,7},{9,8},{10,9},{11,1... | collective-permute-start | bytes 73736 | tf_op jit(solution)/shard_map/ppermute | solution.py:16
  84.5 8.0 %collective-permute-start.5 = (f32[48,128]{1,0:T(8,128)S(1)}, f32[48,128]{1,0:T(8,128)S(1)}, u32[]{:S(2)}, u32[]{:S(2)}) collective-permute-start(f32[48,128]{1,0:T(8,128)S(1)} %get-tuple-element.104), channel_id=1, source_target_pairs={{0,1},{1,2},{2,3},{3,4},{4,5},{5,6},{6,7},{7,8},{8,9},{9,10},{10,1... | collective-permute-start | bytes 73736 | tf_op jit(solution)/shard_map/ppermute | solution.py:16
  92.5 8.6 %collective-permute-start.7 = (f32[128,128]{1,0:T(8,128)S(1)}, f32[128,128]{1,0:T(8,128)S(1)}, u32[]{:S(2)}, u32[]{:S(2)}) collective-permute-start(f32[128,128]{1,0:T(8,128)S(1)} %get-tuple-element.139), channel_id=1, source_target_pairs={{0,16},{16,32},{32,48},{48,64},{64,80},{80,96},{96,112},{112,128},... | collective-permute-start | bytes 196616 | tf_op jit(solution)/shard_map/ppermute | solution.py:16
  94.5 5.5 %collective-permute-start.6 = (f32[128,128]{1,0:T(8,128)S(1)}, f32[128,128]{1,0:T(8,128)S(1)}, u32[]{:S(2)}, u32[]{:S(2)}) collective-permute-start(f32[128,128]{1,0:T(8,128)S(1)} %get-tuple-element.140), channel_id=1, source_target_pairs={{16,0},{32,16},{48,32},{64,48},{80,64},{96,80},{112,96},{128,112},... | collective-permute-start | bytes 196616 | tf_op jit(solution)/shard_map/ppermute | solution.py:16
  99.0 5.3 %copy-start.56 = (s32[288]{0:T(512)S(1)}, s32[288]{0:T(512)}, u32[]{:S(2)}) copy-start(s32[288]{0:T(512)} %copy-done.55) | copy-start | bytes 3460
  350.8 3.0 copy-start.11
  (38 other events, 38.9 us)
Sparse Core Ops, SparseCore 0:
  82.1 268.6 all-reduce.7
where the time goes:
time: 363 us; the launch traced here: 362 us
  waiting for transfers between devices  253 us (70%)
  local copies, waits for them, and re-layouts  47.3 us (13%)
  starting transfers between devices  25.3 us (7%)
  between operations  15.1 us (4%)
  other arithmetic  11.2 us (3%)
  matrix products  10.2 us (3%)
    psum x1, waiting for transfers between devices, local(): sub_grad, down_grad = lax.psum((sub_local, down_local), ('gx', 'gy'))  244 us
    ppermute x4, starting transfers between devices, shifted(): return lax.ppermute(value, axis, pairs)  13.4 us
    unnamed x124, local copies, waits for them, and re-layouts  12.7 us
    dot_general x9, local copies, waits for them, and re-layouts, local(): lax.dot_general(columns, grad_flat, (((0,), (0,)), ((), ())), preferred_e...  9.73 us
    ppermute x2, starting transfers between devices, with_halo(): lax.ppermute(lax.slice_in_dim(block, block.shape[dim] - width, None, axis...  8.65 us
    transpose x10, local copies, waits for them, and re-layouts, local(): jnp.swapaxes(w_sub[first:first + 3], 1, 2).reshape(3 * channels, channels)  8.48 us
  transfers between devices with their start and end apart: 9, of which 5 were waited for; matrix products, arithmetic and copies ran while one was open for 7% of the time, Pallas kernels for 0%

commit v1 on v0

--- a/solution.py
+++ b/solution.py
@@ -187,7 +187,7 @@
             )
     sub_local = jnp.concatenate(weight_parts, 0)
     table_dense = table_dense.reshape(LX + 2, LY + 2, LZ, channels)
-    sub_grad, down_grad = lax.psum((sub_local, down_local), ("gx", "gy"))
+    sub_grad, down_grad = lax.psum(lax.psum((sub_local, down_local), "gx"), "gy")
     ghost_grad = frame_of(table_dense)
     side_grad = ghost_grad[jnp.asarray(frames["side_order"], jnp.int32)]
     grad_west = side_grad[:plane_x]

time: 363 us -> 400 us (1.10)
  waiting for transfers between devices: 253 us -> 293 us
  local copies, waits for them, and re-layouts: 47.3 us -> 42.3 us
    psum x1 -> x2, waiting for transfers between devices: 244 us -> 284 us  [the longest x1 154 us: local(): lax.psum(lax.psum((sub_local, down_local), 'gx'), 'gy')]
    unnamed x124 -> x114, local copies, waits for them, and re-layouts: 12.7 us -> 9.86 us
  transfers between devices with their start and end apart: 9 -> 10, of which waited for: 5 -> 6; matrix products, arithmetic and copies ran while one was open for 7% -> 8% of each run, Pallas kernels for 0% -> 0%
where the time goes in v1:
time: 400 us; the launch traced here: 398 us
  waiting for transfers between devices  293 us (73%)
  local copies, waits for them, and re-layouts  42.3 us (11%)
  starting transfers between devices  24.8 us (6%)
  between operations  15.2 us (4%)
  matrix products  11.2 us (3%)
  other arithmetic  11 us (3%)
    psum x1, waiting for transfers between devices, local(): lax.psum(lax.psum((sub_local, down_local), 'gx'), 'gy')  154 us
    psum x1, waiting for transfers between devices, local(): lax.psum((sub_local, down_local), 'gx')  130 us
    ppermute x4, starting transfers between devices, shifted(): return lax.ppermute(value, axis, pairs)  12.9 us
    unnamed x114, local copies, waits for them, and re-layouts  9.86 us
    transpose x10, local copies, waits for them, and re-layouts, local(): jnp.swapaxes(w_sub[first:first + 3], 1, 2).reshape(3 * channels, channels)  8.99 us
    ppermute x2, starting transfers between devices, with_halo(): lax.ppermute(lax.slice_in_dim(block, block.shape[dim] - width, None, axis...  8.47 us
  transfers between devices with their start and end apart: 10, of which 6 were waited for; matrix products, arithmetic and copies ran while one was open for 8% of the time, Pallas kernels for 0%

profile of v1, /device:TPU:2, one launch (start us, length us, event | category | flops | bytes accessed | tf_op | source)
XLA Modules:
  0.0 397.7 jit_solution(7517634926223583169)
XLA Ops:
  9.4 1.4 gather_fusion
  10.8 1.9 collective-permute-start.1
  12.7 2.4 collective-permute-start
  15.1 2.3 slice_bitcast_fusion.2
  17.8 1.4 scatter_custom_fusion.1
  20.1 1.5 scatter_custom_fusion
  30.3 1.3 collective-permute-start.3
  31.6 6.1 %collective-permute-start.2 = (bf16[3,1,288,128]{3,2,1,0:T(8,128)(2,1)S(1)}, bf16[3,1,288,128]{3,2,1,0:T(8,128)(2,1)S(1)}, u32[]{:S(2)}, u32[]{:S(2)}) collective-permute-start(bf16[3,1,288,128]{3,2,1,0:T(8,128)(2,1)S(1)} %pad_maximum_fusion.19), channel_id=1, source_target_pairs={{0,1},{1,2},{2,3},{3,4},{4,5},{5,6},{6,7},{7,8},{8,9},{9,10},{10,1... | collective-permute-start | bytes 663560 | tf_op jit(solution)/shard_map/ppermute | solution.py:24
  38.3 2.7 collective-permute-done.3
  41.0 4.7 %collective-permute-done.2 = bf16[3,1,288,128]{3,2,1,0:T(8,128)(2,1)S(1)} collective-permute-done((bf16[3,1,288,128]{3,2,1,0:T(8,128)(2,1)S(1)}, bf16[3,1,288,128]{3,2,1,0:T(8,128)(2,1)S(1)}, u32[]{:S(2)}, u32[]{:S(2)}) %collective-permute-start.2) | collective-permute-done | bytes 221216 | tf_op jit(solution)/shard_map/ppermute | solution.py:24
  45.8 1.4 gather_fusion.1
  48.5 1.0 fusion.39
  49.5 1.0 copy.116
  50.5 1.0 copy.112
  55.5 1.4 fusion.8
  62.9 1.3 fusion.47
  64.2 1.3 convolution_dynamic-update-slice_fusion.8
  67.8 1.2 copy-done.1
  69.4 1.0 pad_slice_fusion.1
  74.9 129.8 %all-reduce.12.cloned.1.call-done = (f32[27,128,128]{2,1,0:T(8,128)}, f32[1024,256]{1,0:T(8,128)}) async-done(((f32[27,128,128]{2,1,0:T(8,128)}, f32[1024,256]{1,0:T(8,128)}), (f32[27,128,128]{2,1,0:T(8,128)}, f32[1024,256]{1,0:T(8,128)})) %all-reduce.12.cloned.1.call-update) | async-done | bytes 2818064 | tf_op jit(solution)/shard_map/psum | solution.py:190
  208.1 1.1 gather_fusion.3
  209.2 1.3 collective-permute-start.4
  210.5 6.1 %collective-permute-start.5 = (f32[48,128]{1,0:T(8,128)S(1)}, f32[48,128]{1,0:T(8,128)S(1)}, u32[]{:S(2)}, u32[]{:S(2)}) collective-permute-start(f32[48,128]{1,0:T(8,128)S(1)} %get-tuple-element.106), channel_id=1, source_target_pairs={{0,1},{1,2},{2,3},{3,4},{4,5},{5,6},{6,7},{7,8},{8,9},{9,10},{10,1... | collective-permute-start | bytes 73736 | tf_op jit(solution)/shard_map/ppermute | solution.py:16
  216.6 1.5 collective-permute-done.5
  218.1 1.9 collective-permute-start.7
  220.0 3.6 collective-permute-start.6
  225.6 1.1 scatter_custom_fusion.2
  226.7 1.3 scatter_fusion
  229.9 2.1 scatter_fusion.1
  232.6 154.3 %all-reduce.10.cloned.1.call-done = (f32[27,128,128]{2,1,0:T(8,128)}, f32[1024,256]{1,0:T(8,128)}) async-done(((f32[27,128,128]{2,1,0:T(8,128)}, f32[1024,256]{1,0:T(8,128)}), (f32[27,128,128]{2,1,0:T(8,128)}, f32[1024,256]{1,0:T(8,128)})) %all-reduce.10.cloned.1.call-update) | async-done | bytes 2818064 | tf_op jit(solution)/shard_map/psum | solution.py:190
  386.9 3.0 copy.140
  389.9 1.0 copy.141
  (221 shorter events, 38.2 us)
Async XLA Ops:
  7.2 10.3 %copy-start = (bf16[1024,256]{1,0:T(8,128)(2,1)S(1)}, bf16[1024,256]{1,0:T(8,128)(2,1)}, u32[]{:S(2)}) copy-start(bf16[1024,256]{1,0:T(8,128)(2,1)} %param.28) | copy-start | bytes 1572868
  7.2 197.5 %all-reduce.12.cloned.1.call-start = ((), (), s32[]{:S(2)}) async-start(), calls=%async_computation.1 | async-start | bytes 5636096 | tf_op jit(solution)/shard_map/psum | solution.py:190
  10.8 6.7 %copy-start.42 = (bf16[64,256]{1,0:T(8,128)(2,1)S(1)}, bf16[64,256]{1,0:T(8,128)(2,1)}, u32[]{:S(2)}) copy-start(bf16[64,256]{1,0:T(8,128)(2,1)} %param.31) | copy-start | bytes 98308
  10.8 6.9 %copy-start.55 = (s32[256]{0:T(256)S(1)}, s32[256]{0:T(256)}, u32[]{:S(2)}) copy-start(s32[256]{0:T(256)} %param.29) | copy-start | bytes 3076
  10.8 19.5 %collective-permute-start.1 = (bf16[1,1,288,128]{3,2,1,0:T(8,128)(2,1)S(1)}, bf16[1,1,288,128]{3,2,1,0:T(8,128)(2,1)S(1)}, u32[]{:S(2)}, u32[]{:S(2)}) collective-permute-start(bf16[1,1,288,128]{3,2,1,0:T(8,128)(2,1)S(1)} %bitcast.218), channel_id=1, source_target_pairs={{16,0},{32,16},{48,32},{64,48},{80,64},{96,80},{112,96},{128,112},... | collective-permute-start | bytes 221192 | tf_op jit(solution)/shard_map/ppermute | solution.py:27
  12.7 17.6 %collective-permute-start = (bf16[1,1,288,128]{3,2,1,0:T(8,128)(2,1)S(1)}, bf16[1,1,288,128]{3,2,1,0:T(8,128)(2,1)S(1)}, u32[]{:S(2)}, u32[]{:S(2)}) collective-permute-start(bf16[1,1,288,128]{3,2,1,0:T(8,128)(2,1)S(1)} %bitcast.219), channel_id=1, source_target_pairs={{0,16},{16,32},{32,48},{48,64},{64,80},{80,96},{96,112},{112,128},... | collective-permute-start | bytes 221192 | tf_op jit(solution)/shard_map/ppermute | solution.py:24
  22.7 15.0 %copy-start.53 = (s32[352]{0:T(512)S(1)}, s32[352]{0:T(512)}, u32[]{:S(2)}) copy-start(s32[352]{0:T(512)} %constant.171) | copy-start | bytes 4228
  22.7 15.0 %copy-start.54 = (s32[352]{0:T(512)S(1)}, s32[352]{0:T(512)}, u32[]{:S(2)}) copy-start(s32[352]{0:T(512)} %constant.173) | copy-start | bytes 4228
  30.3 10.7 %collective-permute-start.3 = (bf16[3,1,288,128]{3,2,1,0:T(8,128)(2,1)S(1)}, bf16[3,1,288,128]{3,2,1,0:T(8,128)(2,1)S(1)}, u32[]{:S(2)}, u32[]{:S(2)}) collective-permute-start(bf16[3,1,288,128]{3,2,1,0:T(8,128)(2,1)S(1)} %pad_maximum_fusion.19), channel_id=1, source_target_pairs={{1,0},{2,1},{3,2},{4,3},{5,4},{6,5},{7,6},{8,7},{9,8},{10,9},{11,1... | collective-permute-start | bytes 663560 | tf_op jit(solution)/shard_map/ppermute | solution.py:27
  31.6 14.1 %collective-permute-start.2 = (bf16[3,1,288,128]{3,2,1,0:T(8,128)(2,1)S(1)}, bf16[3,1,288,128]{3,2,1,0:T(8,128)(2,1)S(1)}, u32[]{:S(2)}, u32[]{:S(2)}) collective-permute-start(bf16[3,1,288,128]{3,2,1,0:T(8,128)(2,1)S(1)} %pad_maximum_fusion.19), channel_id=1, source_target_pairs={{0,1},{1,2},{2,3},{3,4},{4,5},{5,6},{6,7},{7,8},{8,9},{9,10},{10,1... | collective-permute-start | bytes 663560 | tf_op jit(solution)/shard_map/ppermute | solution.py:24
  49.4 2.0 copy-start.20
  49.4 2.0 copy-start.22
  49.5 2.0 copy-start.2
  51.5 2.0 copy-start.24
  51.6 1.9 copy-start.25
  55.5 1.7 copy-start.41
  60.5 2.5 copy-start.14
  60.7 2.2 copy-start.43
  62.7 2.9 copy-start.9
  62.9 2.9 copy-start.8
  64.2 1.9 copy-start.10
  64.2 2.2 copy-start.5
  67.8 1.5 copy-start.13
  67.8 1.5 copy-start.15
  67.8 1.5 copy-start.45
  69.0 317.9 %all-reduce.10.cloned.1.call-start = ((), (), s32[]{:S(2)}) async-start(), calls=%async_computation | async-start | bytes 5636096 | tf_op jit(solution)/shard_map/psum | solution.py:190
  209.2 7.4 %collective-permute-start.4 = (f32[48,128]{1,0:T(8,128)S(1)}, f32[48,128]{1,0:T(8,128)S(1)}, u32[]{:S(2)}, u32[]{:S(2)}) collective-permute-start(f32[48,128]{1,0:T(8,128)S(1)} %get-tuple-element.107), channel_id=1, source_target_pairs={{1,0},{2,1},{3,2},{4,3},{5,4},{6,5},{7,6},{8,7},{9,8},{10,9},{11,1... | collective-permute-start | bytes 73736 | tf_op jit(solution)/shard_map/ppermute | solution.py:16
  210.5 7.6 %collective-permute-start.5 = (f32[48,128]{1,0:T(8,128)S(1)}, f32[48,128]{1,0:T(8,128)S(1)}, u32[]{:S(2)}, u32[]{:S(2)}) collective-permute-start(f32[48,128]{1,0:T(8,128)S(1)} %get-tuple-element.106), channel_id=1, source_target_pairs={{0,1},{1,2},{2,3},{3,4},{4,5},{5,6},{6,7},{7,8},{8,9},{9,10},{10,1... | collective-permute-start | bytes 73736 | tf_op jit(solution)/shard_map/ppermute | solution.py:16
  218.1 8.6 %collective-permute-start.7 = (f32[128,128]{1,0:T(8,128)S(1)}, f32[128,128]{1,0:T(8,128)S(1)}, u32[]{:S(2)}, u32[]{:S(2)}) collective-permute-start(f32[128,128]{1,0:T(8,128)S(1)} %get-tuple-element.141), channel_id=1, source_target_pairs={{0,16},{16,32},{32,48},{48,64},{64,80},{80,96},{96,112},{112,128},... | collective-permute-start | bytes 196616 | tf_op jit(solution)/shard_map/ppermute | solution.py:16
  220.0 5.5 %collective-permute-start.6 = (f32[128,128]{1,0:T(8,128)S(1)}, f32[128,128]{1,0:T(8,128)S(1)}, u32[]{:S(2)}, u32[]{:S(2)}) collective-permute-start(f32[128,128]{1,0:T(8,128)S(1)} %get-tuple-element.142), channel_id=1, source_target_pairs={{16,0},{32,16},{48,32},{64,48},{80,64},{96,80},{112,96},{128,112},... | collective-permute-start | bytes 196616 | tf_op jit(solution)/shard_map/ppermute | solution.py:16
  224.5 5.3 %copy-start.51 = (s32[288]{0:T(512)S(1)}, s32[288]{0:T(512)}, u32[]{:S(2)}) copy-start(s32[288]{0:T(512)} %copy-done.50) | copy-start | bytes 3460
  386.9 3.0 copy-start.11
  (34 other events, 34.3 us)
Sparse Core Ops, SparseCore 0:
  69.1 135.5 all-reduce.11
  207.5 179.4 all-reduce.9
